TPU v7x, 256 devices: a whole 4x4x8 slice. The times are simulated.
256 devices in a mesh: noise: 8 (over z), row: 16 (over y, x), col: 2 (over core).
Axes of the slice: x: 4, y: 4, z: 8, core: 2. Of those that a mesh axis runs over, the one named last changes fastest.
Arguments:
- images: bfloat16 [256, 4, 6144], P('row', None, 'col'), may hold values from -40 to 40
- gain: float32 [6144], P('col'), may hold values from 0.3 to 3.5
- up_weight: bfloat16 [6144, 12288], P('col', 'row'), may hold values from -0.078125 to 0.078125
- down_weight: bfloat16 [12288, 6144], P('row', 'col'), may hold values from -0.0546875 to 0.0546875
- cotangent: bfloat16 [256, 16, 6144], P('row', 'noise', 'col'), may hold values from -6 to 6
- seeds: int32 [16], P('noise'), may hold values from 0 to 999999
- assign: int32 [16, 1], replicated, may hold values from 0 to 3, as said below
Outputs:
- saliency: float32 [256, 4, 6144], P('row', None, 'col')
Inputs may be any that keep to these rules, and one draw needn't show every extreme that they name: `assign`: every one of the 4 images is named by at least one copy.
All inputs are finite; a program needn't handle non-finite values.
Results may differ from a plain program's by a relative error of at most 0.0019.
Values may be sent and summed in bfloat16 or wider, within the bound.
A program may use at most 64 MiB of HBM per device.

v0:
```python
import math
import jax
import jax.numpy as jnp
from jax import lax
from jax.sharding import PartitionSpec as P

D = 6144
noise_scale = 0.6
gelu_coef = 0.044715
root_term = math.sqrt(2.0 / math.pi)


def mix_noise(seed_value, token_index, feature_index, width):
    linear = token_index[:, None] * width + feature_index[None, :]
    mixed = linear * 1664525 + seed_value * 1013904223
    mixed = mixed ^ mixed >> 13
    mixed = mixed * 1274126177
    mixed = mixed ^ mixed >> 16
    return ((mixed & 65535).astype(jnp.float32) - 32767.5) * (1.0 / 18918.0)


def gelu_slope(preact):
    inner = root_term * (preact + gelu_coef * preact * preact * preact)
    tanh_val = jnp.tanh(inner)
    return 0.5 * (1.0 + tanh_val) + 0.5 * preact * (1.0 - tanh_val * tanh_val) * root_term * (
        1.0 + 3.0 * gelu_coef * preact * preact
    )


def body(images, gain, up_weight, down_weight, cotangent, seeds, assign):
    slot_count = seeds.shape[0]
    tok_local = images.shape[0]
    image_count = images.shape[1]
    width_local = images.shape[2]
    col_index = lax.axis_index("col")
    row_index = lax.axis_index("row")
    noise_index = lax.axis_index("noise")
    image_ids = jnp.arange(image_count, dtype=jnp.int32)
    my_images = lax.dynamic_slice_in_dim(assign[:, 0], noise_index * slot_count, slot_count)
    onehot = (my_images[:, None] == image_ids[None, :]).astype(jnp.float32)
    clean_rows = jnp.einsum(
        "si,tid->tsd", onehot.astype(jnp.bfloat16), images, preferred_element_type=jnp.float32
    )
    token_index = row_index * tok_local + jnp.arange(tok_local, dtype=jnp.int32)
    feature_index = col_index * width_local + jnp.arange(width_local, dtype=jnp.int32)
    noise_field = jax.vmap(
        lambda seed_value: mix_noise(seed_value, token_index, feature_index, D), out_axes=1
    )(seeds)
    noisy_rows = clean_rows + noise_scale * noise_field
    feat_mean = lax.psum(jnp.sum(noisy_rows, axis=-1), "col") / D
    centred = noisy_rows - feat_mean[..., None]
    feat_var = lax.psum(jnp.sum(centred * centred, axis=-1), "col") / D
    inv_std = lax.rsqrt(feat_var + 1e-06)[..., None]
    normed = centred * inv_std
    scaled = (normed * gain).astype(jnp.bfloat16)
    gathered = (
        lax.all_gather(scaled, "row", axis=0, tiled=True),
        lax.all_gather(cotangent, "row", axis=0, tiled=True),
    )
    row_count = gathered[0].shape[0] * slot_count
    full_scaled = gathered[0].reshape(row_count, width_local)
    full_cotangent = gathered[1].reshape(row_count, width_local)
    preact_part = jnp.dot(full_scaled, up_weight, preferred_element_type=jnp.float32)
    back_part = jnp.einsum(
        "td,hd->th", full_cotangent, down_weight, preferred_element_type=jnp.float32
    )
    preact, back_grad = lax.psum((preact_part, back_part), "col")
    hidden_grad = (back_grad * gelu_slope(preact)).astype(jnp.bfloat16)
    scaled_grad = lax.psum_scatter(
        jnp.einsum("th,dh->td", hidden_grad, up_weight, preferred_element_type=jnp.float32),
        "row",
        scatter_dimension=0,
        tiled=True,
    )
    scaled_grad = scaled_grad.reshape(tok_local, slot_count, width_local)
    normed_grad = scaled_grad * gain
    grad_sum, grad_dot = lax.psum(
        (jnp.sum(normed_grad, axis=-1), jnp.sum(normed_grad * normed, axis=-1)), "col"
    )
    input_grad = cotangent.astype(jnp.float32) + inv_std * (
        normed_grad - grad_sum[..., None] / D - normed * (grad_dot[..., None] / D)
    )
    partial_totals = jnp.einsum("si,tsd->tid", onehot, input_grad, precision=lax.Precision.HIGHEST)
    onehot_all = (assign[:, 0][:, None] == image_ids[None, :]).astype(jnp.float32)
    counts = jnp.sum(onehot_all, axis=0)
    totals = lax.psum(partial_totals, "noise")
    return totals / counts[None, :, None]


def solution(mesh):
    placed = (
        P("row", None, "col"),
        P("col"),
        P("col", "row"),
        P("row", "col"),
        P("row", "noise", "col"),
        P("noise"),
        P(),
    )
    return jax.shard_map(
        body, mesh=mesh, in_specs=placed, out_specs=P("row", None, "col"), check_vma=False
    )
```

profile of v0, /device:TPU:2, one launch (start us, length us, event | category | flops | bytes accessed | tf_op | source)
XLA Modules:
  0.0 361.4 jit_solution(3402559265118721403)
XLA Ops:
  6.5 0.0 copy-start
  6.5 0.0 all-gather.5.cloned.1.call-start
  6.6 0.7 broadcast_multiply_fusion.3
  7.3 0.7 dynamic-slice_bitcast_fusion
  8.0 0.1 add_multiply_fusion
  8.1 0.0 copy-done
  8.1 0.0 copy-start.3
  8.1 0.9 fusion.41
  9.0 2.5 psum.49
  11.5 0.4 multiply_reduce_fusion.2
  11.8 2.5 psum.50
  14.3 0.0 copy-done.3
  14.3 1.0 multiply_convert_fusion
  15.3 0.0 all-gather.5.cloned.1.call-update
  15.3 0.0 all-gather.3.cloned.1.call-start
  15.4 0.7 all-gather.3.cloned.1.call-update
  16.1 0.0 all-reduce.7.cloned.1.call-start
  16.1 54.5 %all-gather.5.cloned.1.call-done = bf16[256,2,3072]{2,1,0:T(2,128)(2,1)} async-done(((bf16[16,2,3072]{2,1,0:T(2,128)(2,1)}), bf16[256,2,3072]{2,1,0:T(2,128)(2,1)}) %all-gather.5.cloned.1.call-update) | async-done | bytes 3145744 | tf_op jit(solution)/shard_map/all_gather | solution.py:57
  70.6 7.5 %reshape.60 = bf16[512,3072]{1,0:T(8,128)(2,1)} reshape(bf16[256,2,3072]{2,1,0:T(2,128)(2,1)} %all-gather.5.cloned.1.call-done) | data formatting | bytes 6291456 | tf_op jit(solution)/shard_map/reshape | solution.py:61
  78.2 7.1 %fusion.43 = f32[512,768]{1,0:T(8,128)} fusion(bf16[512,3072]{1,0:T(8,128)(2,1)} %reshape.60, bf16[3072,768]{1,0:T(8,128)(2,1)} %param.9), kind=kOutput, calls=%fused_computation.66 | convolution fusion | flops 2415919104 | bytes 9437184 | tf_op jit(solution)/shard_map/dot_general | solution.py:63
  85.2 39.8 %all-gather.3.cloned.1.call-done = bf16[256,2,3072]{2,1,0:T(2,128)(2,1)} async-done(((bf16[16,2,3072]{2,1,0:T(2,128)(2,1)}), bf16[256,2,3072]{2,1,0:T(2,128)(2,1)}) %all-gather.3.cloned.1.call-update) | async-done | bytes 3145744 | tf_op jit(solution)/shard_map/all_gather | solution.py:58
  125.0 7.5 %reshape.59 = bf16[512,3072]{1,0:T(8,128)(2,1)} reshape(bf16[256,2,3072]{2,1,0:T(2,128)(2,1)} %all-gather.3.cloned.1.call-done) | data formatting | bytes 6291456 | tf_op jit(solution)/shard_map/reshape | solution.py:62
  132.6 7.1 %fusion.42 = f32[512,768]{1,0:T(8,128)} fusion(bf16[512,3072]{1,0:T(8,128)(2,1)} %reshape.59, bf16[768,3072]{1,0:T(8,128)(2,1)} %param.10), kind=kOutput, calls=%fused_computation.65 | convolution fusion | flops 2415919104 | bytes 9437184 | tf_op jit(solution)/shard_map/td,hd->th/dot_general | solution.py:64
  139.6 0.0 all-reduce.7.cloned.1.call-update
  139.7 0.0 reduce-scatter.2.cloned.1.call-start
  139.7 33.9 %all-reduce.7.cloned.1.call-done = (f32[512,768]{1,0:T(8,128)}, f32[512,768]{1,0:T(8,128)}) async-done(((f32[512,768]{1,0:T(8,128)}, f32[512,768]{1,0:T(8,128)}), (f32[512,768]{1,0:T(8,128)}, f32[512,768]{1,0:T(8,128)})) %all-reduce.7.cloned.1.call-update) | async-done | bytes 3145744 | tf_op jit(solution)/shard_map/psum | solution.py:67
  173.6 9.2 %fusion.8 = f32[512,3072]{1,0:T(8,128)} fusion(bf16[3072,768]{1,0:T(8,128)(2,1)} %param.9, f32[512,768]{1,0:T(8,128)} %get-tuple-element.7, f32[512,768]{1,0:T(8,128)} %get-tuple-element.8), kind=kOutput, calls=%fused_computation.12 | convolution fusion | flops 2423390208 | bytes 14155776 | tf_op jit(solution)/shard_map/th,dh->td/dot_general | solution.py:70
  182.8 0.0 reduce-scatter.2.cloned.1.call-update
  182.8 0.0 copy-start.2
  182.8 0.2 all-reduce.5.cloned.1.call-start
  183.1 87.3 %reduce-scatter.2.cloned.1.call-done = f32[32,3072]{1,0:T(8,128)} async-done(((f32[512,3072]{1,0:T(8,128)}), f32[32,3072]{1,0:T(8,128)}) %reduce-scatter.2.cloned.1.call-update) | async-done | bytes 393232 | tf_op jit(solution)/shard_map/reduce_scatter | solution.py:69
  270.3 0.0 copy-start.1
  270.3 1.3 reshape.61
  271.6 0.5 multiply_reduce_fusion
  272.1 0.0 copy-done.1
  272.1 0.2 multiply_reduce_fusion.1
  272.3 0.1 reduce_sum.50
  272.3 3.3 all-reduce
  275.6 0.0 copy-done.2
  275.7 0.0 copy-start.4
  275.7 2.3 convolution_bitcast_fusion
  278.0 0.0 all-reduce.5.cloned.1.call-update
  278.0 0.0 copy-done.4
  278.0 0.1 convert_reduce_fusion
  278.1 74.4 %all-reduce.5.cloned.1.call-done = f32[16,4,3072]{2,1,0:T(4,128)} async-done(((f32[16,4,3072]{2,1,0:T(4,128)}), f32[16,4,3072]{2,1,0:T(4,128)}) %all-reduce.5.cloned.1.call-update) | async-done | bytes 786448 | tf_op jit(solution)/shard_map/psum | solution.py:86
  352.6 2.3 broadcast_divide_fusion
  (5 shorter events, 0.0 us)
Async XLA Ops:
  6.5 1.5 copy-start
  6.5 64.1 %all-gather.5.cloned.1.call-start = ((), (), s32[]{:S(2)}) async-start(), calls=%async_computation.2 | async-start | bytes 3342336 | tf_op jit(solution)/shard_map/all_gather | solution.py:57
  8.1 6.2 %copy-start.3 = (f32[3072]{0:T(1024)S(1)}, f32[3072]{0:T(1024)}, u32[]{:S(2)}) copy-start(f32[3072]{0:T(1024)} %param.8) | copy-start | bytes 36868
  15.3 109.7 %all-gather.3.cloned.1.call-start = ((), (), s32[]{:S(2)}) async-start(), calls=%async_computation.1 | async-start | bytes 3342336 | tf_op jit(solution)/shard_map/all_gather | solution.py:58
  16.1 157.5 %all-reduce.7.cloned.1.call-start = ((), (), s32[]{:S(2)}) async-start(), calls=%async_computation.5 | async-start | bytes 6291456 | tf_op jit(solution)/shard_map/psum | solution.py:67
  139.7 130.7 %reduce-scatter.2.cloned.1.call-start = ((), (), s32[]{:S(2)}) async-start(), calls=%async_computation.3 | async-start | bytes 6684672 | tf_op jit(solution)/shard_map/reduce_scatter | solution.py:69
  182.8 92.8 %copy-start.2 = (bf16[16,2,3072]{2,1,0:T(2,128)(2,1)S(1)}, bf16[16,2,3072]{2,1,0:T(2,128)(2,1)}, u32[]{:S(2)}) copy-start(bf16[16,2,3072]{2,1,0:T(2,128)(2,1)} %param.11) | copy-start | bytes 589828
  182.8 169.7 %all-reduce.5.cloned.1.call-start = ((), (), s32[]{:S(2)}) async-start(), calls=%async_computation.4 | async-start | bytes 1572864 | tf_op jit(solution)/shard_map/psum | solution.py:86
  270.3 1.8 copy-start.1
  275.7 2.4 copy-start.4
Sparse Core Ops, SparseCore 0:
  15.4 55.1 all-gather.4
  73.1 51.9 all-gather.2
  139.8 33.7 all-reduce.6
  182.9 87.3 reduce-scatter.1
  278.1 74.3 all-reduce.4
where the time goes:
time: 362 us; the launch traced here: 361 us
  waiting for transfers between devices  291 us (80%)
  matrix products  26.6 us (7%)
  local copies, waits for them, and re-layouts  17.2 us (5%)
  between operations  13.2 us (4%)
  blocking collectives  8.21 us (2%)
  other arithmetic  5.16 us (1%)
    reduce_scatter x1, waiting for transfers between devices, body(): lax.psum_scatter(jnp.einsum('th,dh->td', hidden_grad, up_weight, preferre...  87.3 us
    psum x1, waiting for transfers between devices, body(): totals = lax.psum(partial_totals, 'noise')  74.4 us
    all_gather x1, waiting for transfers between devices, body(): lax.all_gather(scaled, 'row', axis=0, tiled=True)  54.5 us
    all_gather x1, waiting for transfers between devices, body(): lax.all_gather(cotangent, 'row', axis=0, tiled=True)  39.8 us
    psum x1, waiting for transfers between devices, body(): preact, back_grad = lax.psum((preact_part, back_part), 'col')  33.9 us
    dot_general x1, matrix products, body(): jnp.einsum('th,dh->td', hidden_grad, up_weight, preferred_element_type=jn...  9.19 us
    reshape x1, local copies, waits for them, and re-layouts, body(): full_scaled = gathered[0].reshape(row_count, width_local)  7.54 us
    reshape x1, local copies, waits for them, and re-layouts, body(): full_cotangent = gathered[1].reshape(row_count, width_local)  7.51 us
  transfers between devices with their start and end apart: 5, of which 5 were waited for; matrix products, arithmetic and copies ran while one was open for 4% of the time, Pallas kernels for 0%

commit v1 on v0

--- a/solution.py
+++ b/solution.py
@@ -53,10 +53,39 @@
     inv_std = lax.rsqrt(feat_var + 1e-06)[..., None]
     normed = centred * inv_std
     scaled = (normed * gain).astype(jnp.bfloat16)
-    gathered = (
-        lax.all_gather(scaled, "row", axis=0, tiled=True),
-        lax.all_gather(cotangent, "row", axis=0, tiled=True),
-    )
+
+    def derive_the_lanes(incoming_x):
+        current_arr, arr_out, z2 = (
+            jax.lax.axis_size("row"),
+            jax.lax.axis_index("row"),
+            incoming_x.shape[0],
+        )
+        panels = tuple(
+            (at * current_arr if ix == 0 else at for ix, at in enumerate(incoming_x.shape))
+        )
+        val2 = lax.dynamic_update_slice_in_dim(
+            jnp.zeros(panels, incoming_x.dtype), incoming_x, arr_out * z2, axis=0
+        )
+        e_now = block_last = incoming_x
+        for jj in tuple(range(1, current_arr // 2 + 1)):
+            e_now = jax.lax.ppermute(
+                e_now, "row", tuple(((ix, (ix + 1) % current_arr) for ix in range(current_arr)))
+            )
+            val2 = lax.dynamic_update_slice_in_dim(
+                val2, e_now, (arr_out - jj) % current_arr * z2, axis=0
+            )
+            if 2 * jj < current_arr:
+                block_last = jax.lax.ppermute(
+                    block_last,
+                    "row",
+                    tuple(((ix, (ix - 1) % current_arr) for ix in range(current_arr))),
+                )
+                val2 = lax.dynamic_update_slice_in_dim(
+                    val2, block_last, (arr_out + jj) % current_arr * z2, axis=0
+                )
+        return val2
+
+    gathered = (derive_the_lanes(scaled), lax.all_gather(cotangent, "row", axis=0, tiled=True))
     row_count = gathered[0].shape[0] * slot_count
     full_scaled = gathered[0].reshape(row_count, width_local)
     full_cotangent = gathered[1].reshape(row_count, width_local)

time: 362 us -> 348 us (0.961)
  waiting for transfers between devices: 291 us -> 241 us
  starting transfers between devices: 0.35 us -> 34.6 us
    all_gather x1 -> x0, waiting for transfers between devices: 54.5 us -> none  [body(): lax.all_gather(scaled, 'row', axis=0, tiled=True)]
    ppermute x0 -> x15, waiting for transfers between devices: none -> 44.2 us  [the longest x8 43.5 us: derive_the_lanes(): jax.lax.ppermute(e_now, 'row', tuple(((ix, (ix + 1) % current_arr) for ix...]
    all_gather x1, waiting for transfers between devices: 39.8 us -> 0.01 us  [body(): lax.all_gather(cotangent, 'row', axis=0, tiled=True)]
    ppermute x0 -> x15, starting transfers between devices: none -> 34.3 us  [the longest x7 31.8 us: derive_the_lanes(): jax.lax.ppermute(block_last, 'row', tuple(((ix, (ix - 1) % current_arr) f...]
    reshape x1, local copies, waits for them, and re-layouts: 7.54 us -> 2.72 us  [body(): full_scaled = gathered[0].reshape(row_count, width_local)]
    dynamic_update_slice x0 -> x15, local copies, waits for them, and re-layouts: none -> 4.18 us  [the longest x8 2.15 us: derive_the_lanes(): lax.dynamic_update_slice_in_dim(val2, e_now, (arr_out - jj) % current_arr...]
  transfers between devices with their start and end apart: 5 -> 19, of which waited for: 5 -> 12; matrix products, arithmetic and copies ran while one was open for 4% -> 4% of each run, Pallas kernels for 0% -> 0%
where the time goes in v1:
time: 348 us; the launch traced here: 347 us
  waiting for transfers between devices  241 us (69%)
  starting transfers between devices  34.6 us (10%)
  matrix products  25.7 us (7%)
  local copies, waits for them, and re-layouts  16.9 us (5%)
  between operations  13.6 us (4%)
  blocking collectives  8.23 us (2%)
  other arithmetic  6.89 us (2%)
    reduce_scatter x1, waiting for transfers between devices, body(): lax.psum_scatter(jnp.einsum('th,dh->td', hidden_grad, up_weight, preferre...  87.5 us
    psum x1, waiting for transfers between devices, body(): totals = lax.psum(partial_totals, 'noise')  74.5 us
    ppermute x8, waiting for transfers between devices, derive_the_lanes(): jax.lax.ppermute(e_now, 'row', tuple(((ix, (ix + 1) % current_arr) for ix...  43.5 us
    psum x1, waiting for transfers between devices, body(): preact, back_grad = lax.psum((preact_part, back_part), 'col')  35.1 us
    ppermute x7, starting transfers between devices, derive_the_lanes(): jax.lax.ppermute(block_last, 'row', tuple(((ix, (ix - 1) % current_arr) f...  31.8 us
    dot_general x1, matrix products, body(): jnp.einsum('th,dh->td', hidden_grad, up_weight, preferred_element_type=jn...  9.23 us
    dot_general x1, matrix products, body(): jnp.dot(full_scaled, up_weight, preferred_element_type=jnp.float32)  7.05 us
  transfers between devices with their start and end apart: 19, of which 12 were waited for; matrix products, arithmetic and copies ran while one was open for 4% of the time, Pallas kernels for 0%

profile of v1, /device:TPU:2, one launch (start us, length us, event | category | flops | bytes accessed | tf_op | source)
XLA Modules:
  0.0 347.2 jit_solution(7968690782528067931)
XLA Ops:
  6.6 0.7 broadcast_multiply_fusion.3
  7.3 0.7 fusion.34
  8.1 0.9 fusion.42
  9.0 2.5 psum.49
  11.5 0.4 multiply_reduce_fusion.2
  11.8 2.5 psum.50
  14.3 1.6 broadcast_in_dim.2
  16.0 1.7 constant_dynamic-update-slice_fusion.15
  17.7 1.5 collective-permute-start
  19.2 0.8 collective-permute-start.1
  20.3 5.2 %collective-permute-done = bf16[16,2,3072]{2,1,0:T(2,128)(2,1)} collective-permute-done((bf16[16,2,3072]{2,1,0:T(2,128)(2,1)}, bf16[16,2,3072]{2,1,0:T(2,128)(2,1)}, u32[]{:S(2)}, u32[]{:S(2)}) %collective-permute-start) | collective-permute-done | bytes 196640 | tf_op jit(solution)/shard_map/ppermute | solution.py:71
  25.5 1.0 collective-permute-start.2
  26.5 4.1 %collective-permute-start.3 = (bf16[16,2,3072]{2,1,0:T(2,128)(2,1)}, bf16[16,2,3072]{2,1,0:T(2,128)(2,1)S(1)}, u32[]{:S(2)}, u32[]{:S(2)}) collective-permute-start(bf16[16,2,3072]{2,1,0:T(2,128)(2,1)} %collective-permute-done.1), channel_id=1, source_target_pairs={{0,30},{2,0},{4,2},{6,4},{8,6},{10,8},{12,10},{14,12},{16,14},{18,... | collective-permute-start | bytes 589832 | tf_op jit(solution)/shard_map/ppermute | solution.py:78
  30.6 1.1 constant_dynamic-update-slice_fusion.14
  31.7 1.1 constant_dynamic-update-slice_fusion.13
  32.8 2.5 collective-permute-done.2
  35.2 5.5 %collective-permute-start.5 = (bf16[16,2,3072]{2,1,0:T(2,128)(2,1)S(1)}, bf16[16,2,3072]{2,1,0:T(2,128)(2,1)S(1)}, u32[]{:S(2)}, u32[]{:S(2)}) collective-permute-start(bf16[16,2,3072]{2,1,0:T(2,128)(2,1)S(1)} %collective-permute-done.3), channel_id=1, source_target_pairs={{0,30},{2,0},{4,2},{6,4},{8,6},{10,8},{12,10},{14,12},{16,14},{18,... | collective-permute-start | bytes 589832 | tf_op jit(solution)/shard_map/ppermute | solution.py:78
  41.0 4.0 %collective-permute-done.4 = bf16[16,2,3072]{2,1,0:T(2,128)(2,1)S(1)} collective-permute-done((bf16[16,2,3072]{2,1,0:T(2,128)(2,1)S(1)}, bf16[16,2,3072]{2,1,0:T(2,128)(2,1)S(1)}, u32[]{:S(2)}, u32[]{:S(2)}) %collective-permute-start.4) | collective-permute-done | bytes 196640 | tf_op jit(solution)/shard_map/ppermute | solution.py:71
  45.0 0.7 collective-permute-done.5
  45.7 5.1 %collective-permute-start.7 = (bf16[16,2,3072]{2,1,0:T(2,128)(2,1)S(1)}, bf16[16,2,3072]{2,1,0:T(2,128)(2,1)S(1)}, u32[]{:S(2)}, u32[]{:S(2)}) collective-permute-start(bf16[16,2,3072]{2,1,0:T(2,128)(2,1)S(1)} %collective-permute-done.5), channel_id=1, source_target_pairs={{0,30},{2,0},{4,2},{6,4},{8,6},{10,8},{12,10},{14,12},{16,14},{18,... | collective-permute-start | bytes 589832 | tf_op jit(solution)/shard_map/ppermute | solution.py:78
  51.0 0.2 constant_dynamic-update-slice_fusion.9
  51.1 3.3 collective-permute-done.6
  54.5 5.3 %collective-permute-start.9 = (bf16[16,2,3072]{2,1,0:T(2,128)(2,1)S(1)}, bf16[16,2,3072]{2,1,0:T(2,128)(2,1)S(1)}, u32[]{:S(2)}, u32[]{:S(2)}) collective-permute-start(bf16[16,2,3072]{2,1,0:T(2,128)(2,1)S(1)} %collective-permute-done.7), channel_id=1, source_target_pairs={{0,30},{2,0},{4,2},{6,4},{8,6},{10,8},{12,10},{14,12},{16,14},{18,... | collective-permute-start | bytes 589832 | tf_op jit(solution)/shard_map/ppermute | solution.py:78
  60.0 0.2 constant_dynamic-update-slice_fusion.7
  60.1 8.0 %collective-permute-done.8 = bf16[16,2,3072]{2,1,0:T(2,128)(2,1)S(1)} collective-permute-done((bf16[16,2,3072]{2,1,0:T(2,128)(2,1)S(1)}, bf16[16,2,3072]{2,1,0:T(2,128)(2,1)S(1)}, u32[]{:S(2)}, u32[]{:S(2)}) %collective-permute-start.8) | collective-permute-done | bytes 196640 | tf_op jit(solution)/shard_map/ppermute | solution.py:71
  68.2 5.4 %collective-permute-start.11 = (bf16[16,2,3072]{2,1,0:T(2,128)(2,1)S(1)}, bf16[16,2,3072]{2,1,0:T(2,128)(2,1)S(1)}, u32[]{:S(2)}, u32[]{:S(2)}) collective-permute-start(bf16[16,2,3072]{2,1,0:T(2,128)(2,1)S(1)} %collective-permute-done.9), channel_id=1, source_target_pairs={{0,30},{2,0},{4,2},{6,4},{8,6},{10,8},{12,10},{14,12},{16,14},{18,... | collective-permute-start | bytes 589832 | tf_op jit(solution)/shard_map/ppermute | solution.py:78
  73.7 0.2 constant_dynamic-update-slice_fusion.5
  73.9 6.7 %collective-permute-done.10 = bf16[16,2,3072]{2,1,0:T(2,128)(2,1)S(1)} collective-permute-done((bf16[16,2,3072]{2,1,0:T(2,128)(2,1)S(1)}, bf16[16,2,3072]{2,1,0:T(2,128)(2,1)S(1)}, u32[]{:S(2)}, u32[]{:S(2)}) %collective-permute-start.10) | collective-permute-done | bytes 196640 | tf_op jit(solution)/shard_map/ppermute | solution.py:71
  80.6 5.7 %collective-permute-start.13 = (bf16[16,2,3072]{2,1,0:T(2,128)(2,1)S(1)}, bf16[16,2,3072]{2,1,0:T(2,128)(2,1)S(1)}, u32[]{:S(2)}, u32[]{:S(2)}) collective-permute-start(bf16[16,2,3072]{2,1,0:T(2,128)(2,1)S(1)} %collective-permute-done.11), channel_id=1, source_target_pairs={{0,30},{2,0},{4,2},{6,4},{8,6},{10,8},{12,10},{14,12},{16,14},{18,... | collective-permute-start | bytes 589832 | tf_op jit(solution)/shard_map/ppermute | solution.py:78
  86.4 0.2 constant_dynamic-update-slice_fusion.3
  86.6 5.3 %collective-permute-done.12 = bf16[16,2,3072]{2,1,0:T(2,128)(2,1)S(1)} collective-permute-done((bf16[16,2,3072]{2,1,0:T(2,128)(2,1)S(1)}, bf16[16,2,3072]{2,1,0:T(2,128)(2,1)S(1)}, u32[]{:S(2)}, u32[]{:S(2)}) %collective-permute-start.12) | collective-permute-done | bytes 196640 | tf_op jit(solution)/shard_map/ppermute | solution.py:71
  92.1 0.2 constant_dynamic-update-slice_fusion.1
  92.2 8.4 %collective-permute-done.14 = bf16[16,2,3072]{2,1,0:T(2,128)(2,1)S(1)} collective-permute-done((bf16[16,2,3072]{2,1,0:T(2,128)(2,1)S(1)}, bf16[16,2,3072]{2,1,0:T(2,128)(2,1)S(1)}, u32[]{:S(2)}, u32[]{:S(2)}) %collective-permute-start.14) | collective-permute-done | bytes 196640 | tf_op jit(solution)/shard_map/ppermute | solution.py:71
  100.8 2.7 reshape.60
  103.5 7.0 %fusion.44 = f32[512,768]{1,0:T(8,128)} fusion(bf16[512,3072]{1,0:T(8,128)(2,1)} %reshape.60, bf16[3072,768]{1,0:T(8,128)(2,1)} %param.9), kind=kOutput, calls=%fused_computation.83 | convolution fusion | flops 2415919104 | bytes 9437184 | tf_op jit(solution)/shard_map/dot_general | solution.py:92
  110.5 6.3 %reshape.59 = bf16[512,3072]{1,0:T(8,128)(2,1)S(1)} reshape(bf16[256,2,3072]{2,1,0:T(2,128)(2,1)} %all-gather.2.cloned.1.call-done) | data formatting | bytes 6291456 | tf_op jit(solution)/shard_map/reshape | solution.py:91
  116.9 6.2 %fusion.43 = f32[512,768]{1,0:T(8,128)} fusion(bf16[512,3072]{1,0:T(8,128)(2,1)S(1)} %reshape.59, bf16[768,3072]{1,0:T(8,128)(2,1)} %param.10), kind=kOutput, calls=%fused_computation.82 | convolution fusion | flops 2415919104 | bytes 9437184 | tf_op jit(solution)/shard_map/td,hd->th/dot_general | solution.py:93
  123.1 0.3 reduce-scatter.2.cloned.1.call-start
  123.3 35.1 %all-reduce.7.cloned.1.call-done = (f32[512,768]{1,0:T(8,128)}, f32[512,768]{1,0:T(8,128)}) async-done(((f32[512,768]{1,0:T(8,128)}, f32[512,768]{1,0:T(8,128)}), (f32[512,768]{1,0:T(8,128)}, f32[512,768]{1,0:T(8,128)})) %all-reduce.7.cloned.1.call-update) | async-done | bytes 3145744 | tf_op jit(solution)/shard_map/psum | solution.py:96
  158.5 9.2 %fusion.8 = f32[512,3072]{1,0:T(8,128)} fusion(bf16[3072,768]{1,0:T(8,128)(2,1)} %param.9, f32[512,768]{1,0:T(8,128)} %get-tuple-element.7, f32[512,768]{1,0:T(8,128)} %get-tuple-element.8), kind=kOutput, calls=%fused_computation.12 | convolution fusion | flops 2423390208 | bytes 14155776 | tf_op jit(solution)/shard_map/th,dh->td/dot_general | solution.py:99
  167.8 87.5 %reduce-scatter.2.cloned.1.call-done = f32[32,3072]{1,0:T(8,128)} async-done(((f32[512,3072]{1,0:T(8,128)}), f32[32,3072]{1,0:T(8,128)}) %reduce-scatter.2.cloned.1.call-update) | async-done | bytes 393232 | tf_op jit(solution)/shard_map/reduce_scatter | solution.py:98
  255.3 1.2 reshape.61
  256.5 0.5 multiply_reduce_fusion
  257.0 1.1 multiply_reduce_fusion.1
  258.2 3.3 all-reduce
  261.5 2.3 convolution_bitcast_fusion
  264.0 74.5 %all-reduce.5.cloned.1.call-done = f32[16,4,3072]{2,1,0:T(4,128)} async-done(((f32[16,4,3072]{2,1,0:T(4,128)}), f32[16,4,3072]{2,1,0:T(4,128)}) %all-reduce.5.cloned.1.call-update) | async-done | bytes 786448 | tf_op jit(solution)/shard_map/psum | solution.py:115
  338.4 2.3 broadcast_divide_fusion
  (54 shorter events, 1.8 us)
Async XLA Ops:
  6.5 1.5 copy-start
  6.5 104.0 %all-gather.2.cloned.1.call-start = ((), (), s32[]{:S(2)}) async-start(), calls=%async_computation.1 | async-start | bytes 3342336 | tf_op jit(solution)/shard_map/all_gather | solution.py:88
  8.1 6.2 %copy-start.7 = (s32[2]{0:T(128)}, s32[2]{0:T(128)S(1)}, u32[]{:S(2)}) copy-start(s32[2]{0:T(128)S(1)} %fusion.34) | copy-start | bytes 28
  9.0 5.3 %copy-start.1 = (f32[16,2,3072]{2,1,0:T(2,128)}, f32[16,2,3072]{2,1,0:T(2,128)S(1)}, u32[]{:S(2)}) copy-start(f32[16,2,3072]{2,1,0:T(2,128)S(1)} %get-tuple-element.12) | copy-start | bytes 1179652
  14.3 1.6 copy-start.2
  17.7 7.8 %collective-permute-start = (bf16[16,2,3072]{2,1,0:T(2,128)(2,1)}, bf16[16,2,3072]{2,1,0:T(2,128)(2,1)}, u32[]{:S(2)}, u32[]{:S(2)}) collective-permute-start(bf16[16,2,3072]{2,1,0:T(2,128)(2,1)} %get-tuple-element.10), channel_id=1, source_target_pairs={{0,2},{2,4},{4,6},{6,8},{8,10},{10,12},{12,14},{14,16},{16,18},{18... | collective-permute-start | bytes 589832 | tf_op jit(solution)/shard_map/ppermute | solution.py:71
  19.2 7.3 %collective-permute-start.1 = (bf16[16,2,3072]{2,1,0:T(2,128)(2,1)}, bf16[16,2,3072]{2,1,0:T(2,128)(2,1)}, u32[]{:S(2)}, u32[]{:S(2)}) collective-permute-start(bf16[16,2,3072]{2,1,0:T(2,128)(2,1)} %get-tuple-element.10), channel_id=1, source_target_pairs={{0,30},{2,0},{4,2},{6,4},{8,6},{10,8},{12,10},{14,12},{16,14},{18,... | collective-permute-start | bytes 589832 | tf_op jit(solution)/shard_map/ppermute | solution.py:78
  20.0 138.5 %all-reduce.7.cloned.1.call-start = ((), (), s32[]{:S(2)}) async-start(), calls=%async_computation.4 | async-start | bytes 6291456 | tf_op jit(solution)/shard_map/psum | solution.py:96
  25.5 9.7 %collective-permute-start.2 = (bf16[16,2,3072]{2,1,0:T(2,128)(2,1)}, bf16[16,2,3072]{2,1,0:T(2,128)(2,1)S(1)}, u32[]{:S(2)}, u32[]{:S(2)}) collective-permute-start(bf16[16,2,3072]{2,1,0:T(2,128)(2,1)} %collective-permute-done), channel_id=1, source_target_pairs={{0,2},{2,4},{4,6},{6,8},{8,10},{10,12},{12,14},{14,16},{16,18},{18... | collective-permute-start | bytes 589832 | tf_op jit(solution)/shard_map/ppermute | solution.py:71
  26.5 8.7 %collective-permute-start.3 = (bf16[16,2,3072]{2,1,0:T(2,128)(2,1)}, bf16[16,2,3072]{2,1,0:T(2,128)(2,1)S(1)}, u32[]{:S(2)}, u32[]{:S(2)}) collective-permute-start(bf16[16,2,3072]{2,1,0:T(2,128)(2,1)} %collective-permute-done.1), channel_id=1, source_target_pairs={{0,30},{2,0},{4,2},{6,4},{8,6},{10,8},{12,10},{14,12},{16,14},{18,... | collective-permute-start | bytes 589832 | tf_op jit(solution)/shard_map/ppermute | solution.py:78
  35.2 9.8 %collective-permute-start.4 = (bf16[16,2,3072]{2,1,0:T(2,128)(2,1)S(1)}, bf16[16,2,3072]{2,1,0:T(2,128)(2,1)S(1)}, u32[]{:S(2)}, u32[]{:S(2)}) collective-permute-start(bf16[16,2,3072]{2,1,0:T(2,128)(2,1)S(1)} %collective-permute-done.2), channel_id=1, source_target_pairs={{0,2},{2,4},{4,6},{6,8},{8,10},{10,12},{12,14},{14,16},{16,18},{18... | collective-permute-start | bytes 589832 | tf_op jit(solution)/shard_map/ppermute | solution.py:71
  35.2 10.5 %collective-permute-start.5 = (bf16[16,2,3072]{2,1,0:T(2,128)(2,1)S(1)}, bf16[16,2,3072]{2,1,0:T(2,128)(2,1)S(1)}, u32[]{:S(2)}, u32[]{:S(2)}) collective-permute-start(bf16[16,2,3072]{2,1,0:T(2,128)(2,1)S(1)} %collective-permute-done.3), channel_id=1, source_target_pairs={{0,30},{2,0},{4,2},{6,4},{8,6},{10,8},{12,10},{14,12},{16,14},{18,... | collective-permute-start | bytes 589832 | tf_op jit(solution)/shard_map/ppermute | solution.py:78
  45.0 9.4 %collective-permute-start.6 = (bf16[16,2,3072]{2,1,0:T(2,128)(2,1)S(1)}, bf16[16,2,3072]{2,1,0:T(2,128)(2,1)S(1)}, u32[]{:S(2)}, u32[]{:S(2)}) collective-permute-start(bf16[16,2,3072]{2,1,0:T(2,128)(2,1)S(1)} %collective-permute-done.4), channel_id=1, source_target_pairs={{0,2},{2,4},{4,6},{6,8},{8,10},{10,12},{12,14},{14,16},{16,18},{18... | collective-permute-start | bytes 589832 | tf_op jit(solution)/shard_map/ppermute | solution.py:71
  45.7 8.7 %collective-permute-start.7 = (bf16[16,2,3072]{2,1,0:T(2,128)(2,1)S(1)}, bf16[16,2,3072]{2,1,0:T(2,128)(2,1)S(1)}, u32[]{:S(2)}, u32[]{:S(2)}) collective-permute-start(bf16[16,2,3072]{2,1,0:T(2,128)(2,1)S(1)} %collective-permute-done.5), channel_id=1, source_target_pairs={{0,30},{2,0},{4,2},{6,4},{8,6},{10,8},{12,10},{14,12},{16,14},{18,... | collective-permute-start | bytes 589832 | tf_op jit(solution)/shard_map/ppermute | solution.py:78
  54.5 13.7 %collective-permute-start.8 = (bf16[16,2,3072]{2,1,0:T(2,128)(2,1)S(1)}, bf16[16,2,3072]{2,1,0:T(2,128)(2,1)S(1)}, u32[]{:S(2)}, u32[]{:S(2)}) collective-permute-start(bf16[16,2,3072]{2,1,0:T(2,128)(2,1)S(1)} %collective-permute-done.6), channel_id=1, source_target_pairs={{0,2},{2,4},{4,6},{6,8},{8,10},{10,12},{12,14},{14,16},{16,18},{18... | collective-permute-start | bytes 589832 | tf_op jit(solution)/shard_map/ppermute | solution.py:71
  54.5 13.7 %collective-permute-start.9 = (bf16[16,2,3072]{2,1,0:T(2,128)(2,1)S(1)}, bf16[16,2,3072]{2,1,0:T(2,128)(2,1)S(1)}, u32[]{:S(2)}, u32[]{:S(2)}) collective-permute-start(bf16[16,2,3072]{2,1,0:T(2,128)(2,1)S(1)} %collective-permute-done.7), channel_id=1, source_target_pairs={{0,30},{2,0},{4,2},{6,4},{8,6},{10,8},{12,10},{14,12},{16,14},{18,... | collective-permute-start | bytes 589832 | tf_op jit(solution)/shard_map/ppermute | solution.py:78
  68.2 12.4 %collective-permute-start.10 = (bf16[16,2,3072]{2,1,0:T(2,128)(2,1)S(1)}, bf16[16,2,3072]{2,1,0:T(2,128)(2,1)S(1)}, u32[]{:S(2)}, u32[]{:S(2)}) collective-permute-start(bf16[16,2,3072]{2,1,0:T(2,128)(2,1)S(1)} %collective-permute-done.8), channel_id=1, source_target_pairs={{0,2},{2,4},{4,6},{6,8},{8,10},{10,12},{12,14},{14,16},{16,18},{18... | collective-permute-start | bytes 589832 | tf_op jit(solution)/shard_map/ppermute | solution.py:71
  68.2 12.4 %collective-permute-start.11 = (bf16[16,2,3072]{2,1,0:T(2,128)(2,1)S(1)}, bf16[16,2,3072]{2,1,0:T(2,128)(2,1)S(1)}, u32[]{:S(2)}, u32[]{:S(2)}) collective-permute-start(bf16[16,2,3072]{2,1,0:T(2,128)(2,1)S(1)} %collective-permute-done.9), channel_id=1, source_target_pairs={{0,30},{2,0},{4,2},{6,4},{8,6},{10,8},{12,10},{14,12},{16,14},{18,... | collective-permute-start | bytes 589832 | tf_op jit(solution)/shard_map/ppermute | solution.py:78
  80.6 11.3 %collective-permute-start.12 = (bf16[16,2,3072]{2,1,0:T(2,128)(2,1)S(1)}, bf16[16,2,3072]{2,1,0:T(2,128)(2,1)S(1)}, u32[]{:S(2)}, u32[]{:S(2)}) collective-permute-start(bf16[16,2,3072]{2,1,0:T(2,128)(2,1)S(1)} %collective-permute-done.10), channel_id=1, source_target_pairs={{0,2},{2,4},{4,6},{6,8},{8,10},{10,12},{12,14},{14,16},{16,18},{18... | collective-permute-start | bytes 589832 | tf_op jit(solution)/shard_map/ppermute | solution.py:71
  80.6 11.5 %collective-permute-start.13 = (bf16[16,2,3072]{2,1,0:T(2,128)(2,1)S(1)}, bf16[16,2,3072]{2,1,0:T(2,128)(2,1)S(1)}, u32[]{:S(2)}, u32[]{:S(2)}) collective-permute-start(bf16[16,2,3072]{2,1,0:T(2,128)(2,1)S(1)} %collective-permute-done.11), channel_id=1, source_target_pairs={{0,30},{2,0},{4,2},{6,4},{8,6},{10,8},{12,10},{14,12},{16,14},{18,... | collective-permute-start | bytes 589832 | tf_op jit(solution)/shard_map/ppermute | solution.py:78
  91.9 8.7 %collective-permute-start.14 = (bf16[16,2,3072]{2,1,0:T(2,128)(2,1)S(1)}, bf16[16,2,3072]{2,1,0:T(2,128)(2,1)S(1)}, u32[]{:S(2)}, u32[]{:S(2)}) collective-permute-start(bf16[16,2,3072]{2,1,0:T(2,128)(2,1)S(1)} %collective-permute-done.12), channel_id=1, source_target_pairs={{0,2},{2,4},{4,6},{6,8},{8,10},{10,12},{12,14},{14,16},{16,18},{18... | collective-permute-start | bytes 589832 | tf_op jit(solution)/shard_map/ppermute | solution.py:71
  123.1 132.2 %reduce-scatter.2.cloned.1.call-start = ((), (), s32[]{:S(2)}) async-start(), calls=%async_computation.2 | async-start | bytes 6684672 | tf_op jit(solution)/shard_map/reduce_scatter | solution.py:98
  167.7 88.8 %copy-start.3 = (f32[16,2,3072]{2,1,0:T(2,128)S(1)}, f32[16,2,3072]{2,1,0:T(2,128)}, u32[]{:S(2)}) copy-start(f32[16,2,3072]{2,1,0:T(2,128)} %copy-done.1) | copy-start | bytes 1179652
  167.7 88.8 %copy-start.5 = (f32[3072]{0:T(1024)S(1)}, f32[3072]{0:T(1024)}, u32[]{:S(2)}) copy-start(f32[3072]{0:T(1024)} %param.8) | copy-start | bytes 36868
  167.7 93.8 %copy-start.4 = (bf16[16,2,3072]{2,1,0:T(2,128)(2,1)S(1)}, bf16[16,2,3072]{2,1,0:T(2,128)(2,1)}, u32[]{:S(2)}) copy-start(bf16[16,2,3072]{2,1,0:T(2,128)(2,1)} %param.11) | copy-start | bytes 589828
  167.7 93.8 %copy-start.8 = (s32[2]{0:T(128)S(1)}, s32[2]{0:T(128)}, u32[]{:S(2)}) copy-start(s32[2]{0:T(128)} %copy-done.7) | copy-start | bytes 28
  167.7 96.1 %copy-start.6 = (s32[16,1]{0,1:T(1,128)S(1)}, s32[16,1]{0,1:T(1,128)}, u32[]{:S(2)}) copy-start(s32[16,1]{0,1:T(1,128)} %param.13) | copy-start | bytes 196
  167.8 170.7 %all-reduce.5.cloned.1.call-start = ((), (), s32[]{:S(2)}) async-start(), calls=%async_computation.3 | async-start | bytes 1572864 | tf_op jit(solution)/shard_map/psum | solution.py:115
Sparse Core Ops, SparseCore 0:
  20.1 61.2 all-gather.1
  123.2 35.2 all-reduce.6
  167.9 87.3 reduce-scatter.1
  264.0 74.4 all-reduce.4
